TPU v7x, 32 devices: a whole 2x2x4 slice. The times are simulated.
32 devices in a mesh: dom: 8 (over z, x), tp: 4 (over y, core).
Axes of the slice: x: 2, y: 2, z: 4, core: 2. Of those that a mesh axis runs over, the one named last changes fastest.
Arguments:
- hidden: bfloat16 [4, 8, 256, 8192], P(None, 'dom', None, 'tp')
- fc2_weight: bfloat16 [8192, 8192], P('tp')
- fc2_bias: bfloat16 [8192], replicated, may hold values from -6 to 6
- norm_gain: bfloat16 [8192], replicated, may hold values from 0.099609375 to 1.8984375
- kv_weight: bfloat16 [8192, 2048], P('tp'), may hold values from -0.09375 to 0.09375
- kv_bias: bfloat16 [2048], replicated, may hold values from -3 to 3
- tiles_per_request: int32 [16], replicated, may hold values from 0 to 8, as said below
- request_group: int32 [16], replicated, may hold values from 0 to 7, as said below
- text_lengths: int32 [16], replicated, may hold values from 16 to 2047
Outputs:
- kv_cache: bfloat16 [16384, 2048], P('dom', 'tp')
Inputs may be any that keep to these rules, and one draw needn't show every extreme that they name: `tiles_per_request`: sums to 32; the requests of one prefill group hold at most 8 tiles together, and some group holds exactly that many. `request_group`: never falls from one request to the next; every prefill group has at least one request.
All inputs are finite; a program needn't handle non-finite values.
Results may differ from a plain program's by a relative error of at most 0.017.
Values may be sent and summed in bfloat16 or wider, within the bound.
A program may use at most 192 MiB of HBM per device.

v0:
```python
import jax
import jax.numpy as jnp
from jax import lax
from jax.sharding import PartitionSpec as P

HEAD = 128


EPS = 1e-06
ROPE_BASE = 1000000.0


def tile_plan(tiles_per_request, request_group, text_lengths, tile_count, group_count, rows_tile):
    request_count = tiles_per_request.shape[0]
    ends = jnp.cumsum(tiles_per_request)
    starts = ends - tiles_per_request
    tile_ids = jnp.arange(tile_count, dtype=jnp.int32)
    owner = jnp.sum((ends[None, :] <= tile_ids[:, None]).astype(jnp.int32), axis=1)
    member = (owner[:, None] == jnp.arange(request_count, dtype=jnp.int32)[None, :]).astype(
        jnp.int32
    )
    start_of = jnp.sum(member * starts[None, :], axis=1)
    group_of = jnp.sum(member * request_group[None, :], axis=1)
    text_of = jnp.sum(member * text_lengths[None, :], axis=1)
    group_ids = jnp.arange(group_count, dtype=jnp.int32)
    same_group = (request_group[None, :] == group_ids[:, None]).astype(jnp.int32)
    below_group = (request_group[None, :] < group_ids[:, None]).astype(jnp.int32)
    counts = jnp.sum(same_group * tiles_per_request[None, :], axis=1)
    firsts = jnp.sum(below_group * tiles_per_request[None, :], axis=1)
    first_of = jnp.sum(
        (group_of[:, None] == group_ids[None, :]).astype(jnp.int32) * firsts[None, :], axis=1
    )
    slot_of = tile_ids - first_of
    base_of = text_of + (tile_ids - start_of) * rows_tile
    return (group_of, slot_of, base_of, counts, firsts)


def rotate_heads(values, positions, head_size):
    row_count, col_count = values.shape
    grid = values.reshape(row_count, col_count // head_size, head_size)
    half_size = head_size // 2
    freqs = ROPE_BASE ** (-jnp.arange(half_size, dtype=jnp.float32) * 2.0 / head_size)
    angles = positions.astype(jnp.float32)[:, None] * freqs[None, :]
    cosine = jnp.concatenate([jnp.cos(angles), jnp.cos(angles)], axis=1)[:, None, :]
    sine = jnp.concatenate([jnp.sin(angles), jnp.sin(angles)], axis=1)[:, None, :]
    turned = jnp.concatenate([-grid[..., half_size:], grid[..., :half_size]], axis=-1)
    return (grid * cosine + turned * sine).reshape(row_count, col_count)


def lookup(table, wanted):
    table_ids = jnp.arange(table.shape[0], dtype=jnp.int32)
    hits = (wanted[:, None] == table_ids[None, :]).astype(jnp.int32)
    return jnp.sum(hits * table[None, :], axis=1)


def pick_rows(picker, payload):
    return jnp.dot(picker, payload, preferred_element_type=jnp.float32).astype(jnp.bfloat16)


def finish_cache(summed, kv_bias, positions, lane_index, lane_cols, cache_cols):
    bias_part = lax.dynamic_slice_in_dim(kv_bias, lane_index * lane_cols, lane_cols).astype(
        jnp.float32
    )
    raw = summed + bias_part[None, :]
    turned = rotate_heads(raw, positions, HEAD)
    is_key = lane_index * lane_cols < cache_cols // 2
    return jnp.where(is_key, turned, raw).astype(jnp.bfloat16)


def body(
    hidden,
    fc2_weight,
    fc2_bias,
    norm_gain,
    kv_weight,
    kv_bias,
    tiles_per_request,
    request_group,
    text_lengths,
):
    group_count = lax.axis_size("dom")
    lane_count = lax.axis_size("tp")
    group_index = lax.axis_index("dom")
    lane_index = lax.axis_index("tp")
    local_tiles = hidden.shape[0]
    rows_tile = hidden.shape[2]
    local_width = hidden.shape[3]
    model_width = fc2_weight.shape[1]
    cache_cols = kv_weight.shape[1]
    lane_cols = cache_cols // lane_count
    pre_tiles = 2 * local_tiles
    tile_count = local_tiles * group_count
    group_of, slot_of, base_of, counts, firsts = tile_plan(
        tiles_per_request, request_group, text_lengths, tile_count, group_count, rows_tile
    )
    tile_rows = hidden.reshape(local_tiles * rows_tile, local_width)
    partial_value = jnp.dot(tile_rows, fc2_weight, preferred_element_type=jnp.float32).reshape(
        local_tiles, rows_tile, model_width
    )
    summed_cols = lax.psum_scatter(
        partial_value.astype(jnp.bfloat16), "tp", scatter_dimension=2, tiled=True
    ).astype(jnp.float32)
    bias_part = lax.dynamic_slice_in_dim(fc2_bias, lane_index * local_width, local_width).astype(
        jnp.float32
    )
    gain_part = lax.dynamic_slice_in_dim(norm_gain, lane_index * local_width, local_width).astype(
        jnp.float32
    )
    projected = (summed_cols + bias_part[None, None, :]).astype(jnp.bfloat16)
    widened = projected.astype(jnp.float32)
    squares = lax.psum(jnp.sum(widened * widened, axis=2), "tp")
    scale = lax.rsqrt(squares / model_width + EPS)[..., None]
    normed = (widened * scale * gain_part[None, None, :]).astype(jnp.bfloat16)
    group_ids = jnp.arange(group_count, dtype=jnp.int32)
    mine = jnp.arange(local_tiles, dtype=jnp.int32) * group_count + group_index
    mine_group = lookup(group_of, mine)
    send_picker = (group_ids[:, None] == mine_group[None, :]).astype(jnp.bfloat16)
    slot_ids = jnp.arange(pre_tiles, dtype=jnp.int32)
    my_count = lookup(counts, jnp.full((1,), group_index, jnp.int32))[0]
    my_first = lookup(firsts, jnp.full((1,), group_index, jnp.int32))[0]
    wanted = my_first + slot_ids
    valid = slot_ids < my_count
    source = wanted % group_count
    take_picker = jnp.logical_and(source[:, None] == group_ids[None, :], valid[:, None]).astype(
        jnp.bfloat16
    )
    row_ids = jnp.arange(rows_tile, dtype=jnp.int32)
    partial_kv = jnp.dot(
        normed.reshape(local_tiles * rows_tile, local_width),
        kv_weight,
        preferred_element_type=jnp.float32,
    )
    summed_kv = lax.psum_scatter(
        partial_kv.astype(jnp.bfloat16), "tp", scatter_dimension=1, tiled=True
    ).astype(jnp.float32)
    mine_positions = (lookup(base_of, mine)[:, None] + row_ids[None, :]).reshape(
        local_tiles * rows_tile
    )
    cache = finish_cache(summed_kv, kv_bias, mine_positions, lane_index, lane_cols, cache_cols)
    outgoing = pick_rows(send_picker, cache.reshape(local_tiles, rows_tile * lane_cols))
    arrived = lax.all_to_all(
        outgoing.reshape(group_count, rows_tile, lane_cols),
        "dom",
        split_axis=0,
        concat_axis=0,
        tiled=True,
    )
    placed = pick_rows(take_picker, arrived.reshape(group_count, rows_tile * lane_cols))
    return placed.reshape(pre_tiles * rows_tile, lane_cols)


def solution(mesh):
    return jax.shard_map(
        body,
        mesh=mesh,
        in_specs=(
            P(None, "dom", None, "tp"),
            P("tp", None),
            P(),
            P(),
            P("tp", None),
            P(),
            P(),
            P(),
            P(),
        ),
        out_specs=P("dom", "tp"),
        check_vma=False,
    )
```

profile of v0, /device:TPU:0, one launch (start us, length us, event | category | flops | bytes accessed | tf_op | source)
XLA Modules:
  0.0 324.3 jit_solution(6656410311374316671)
XLA Ops:
  6.5 41.8 %fusion.2 = bf16[4,256,8192]{2,1,0:T(8,128)(2,1)} fusion(bf16[2048,8192]{1,0:T(8,128)(2,1)} %param.10, bf16[4,1,256,2048]{3,2,1,0:T(8,128)(2,1)} %param.9), kind=kOutput, calls=%fused_computation.4 | convolution fusion | flops 34368126976 | bytes 54525952 | tf_op jit(solution)/shard_map/dot_general | solution.py:97
  48.4 0.7 dynamic-slice_convert_fusion.1
  49.1 0.7 dynamic-slice_convert_fusion
  49.8 127.6 %reduce-scatter.3.cloned.1.call-done = bf16[4,256,2048]{2,1,0:T(8,128)(2,1)} async-done(((bf16[4,256,8192]{2,1,0:T(8,128)(2,1)}), bf16[4,256,2048]{2,1,0:T(8,128)(2,1)}) %reduce-scatter.3.cloned.1.call-update) | async-done | bytes 4194320 | tf_op jit(solution)/shard_map/reduce_scatter | solution.py:100
  177.4 3.3 %fusion.5 = f32[4,256]{1,0:T(4,128)S(1)} fusion(f32[2048]{0:T(1024)S(1)} %dynamic-slice_convert_fusion.1, bf16[4,256,2048]{2,1,0:T(8,128)(2,1)} %reduce-scatter.3.cloned.1.call-done), kind=kLoop, calls=%fused_computation.7 | loop fusion | flops 12581888 | bytes 4206592 | tf_op jit(solution)/shard_map/reduce_sum | solution.py:111
  180.7 5.8 %psum.7 = f32[4,256]{1,0:T(4,128)S(1)} all-reduce(f32[4,256]{1,0:T(4,128)S(1)} %fusion.5), channel_id=1, replica_groups=mesh['dom'=8,'tp'=4] {'tp'}, use_global_device_ids=true, to_apply=%region_10.11 | all-reduce | flops 1024 | bytes 8192 | tf_op jit(solution)/shard_map/psum | solution.py:111
  186.5 3.6 %fusion.7 = bf16[4,256,2048]{2,1,0:T(8,128)(2,1)S(1)} fusion(f32[2048]{0:T(1024)S(1)} %dynamic-slice_convert_fusion, f32[4,256]{1,0:T(4,128)S(1)} %add_rsqrt_fusion, f32[2048]{0:T(1024)S(1)} %dynamic-slice_convert_fusion.1, bf16[4,256,2048]{2,1,0:T(8,128)(2,1)} %reduce-scatter.3.cloned.1.call-done), kind=kLoop, calls=%fused_computation.9 | loop fusion | flops 14680064 | bytes 8409088 | tf_op jit(solution)/shard_map/convert_element_type | solution.py:113
  190.1 1.1 copy-done.4
  191.1 10.5 %convolution_convert_fusion.2 = bf16[1024,2048]{1,0:T(8,128)(2,1)} fusion(bf16[1024,2048]{1,0:T(8,128)(2,1)S(1)} %bitcast.37, bf16[2048,2048]{1,0:T(8,128)(2,1)S(1)} %copy-done.4), kind=kOutput, calls=%fused_computation.12 | convolution fusion | flops 8592031744 | bytes 16777216 | tf_op jit(solution)/shard_map/dot_general | solution.py:128
  201.7 0.6 copy-done.2
  202.8 0.2 select_reduce_fusion.6
  203.0 0.8 dynamic-slice_convert_fusion.2
  203.8 1.9 multiply_cosine_fusion
  205.7 0.3 pad_maximum_fusion
  206.0 41.4 %reduce-scatter.5.cloned.1.call-done = bf16[1024,512]{1,0:T(8,128)(2,1)} async-done(((bf16[1024,2048]{1,0:T(8,128)(2,1)}), bf16[1024,512]{1,0:T(8,128)(2,1)}) %reduce-scatter.5.cloned.1.call-update) | async-done | bytes 1048592 | tf_op jit(solution)/shard_map/reduce_scatter | solution.py:133
  247.4 2.8 convert_add_fusion
  250.3 2.2 reshape.137
  252.4 1.2 slice_negate_fusion
  253.7 1.2 maximum_multiply_fusion
  254.9 0.4 mul.171
  255.3 0.7 fusion.10
  256.0 0.8 reshape.138
  256.8 0.7 convolution_convert_fusion.1
  257.5 2.0 copy.15
  259.5 5.5 %all-to-all-start = ((bf16[8,256,512]{2,1,0:T(8,128)(2,1)}), bf16[8,256,512]{2,1,0:T(8,128)(2,1)S(1)}, u32[]{:S(2)}, u32[]{:S(2)}) async-start(bf16[8,256,512]{2,1,0:T(8,128)(2,1)} %copy.15), calls=%async_computation.2 | async-start | bytes 4194304 | tf_op jit(solution)/shard_map/all_to_all | solution.py:141
  265.2 0.7 fusion.16
  265.9 0.7 and_select_fusion
  266.6 0.6 iota_compare_fusion.8
  267.1 46.1 %all-to-all-done = bf16[8,256,512]{2,1,0:T(8,128)(2,1)S(1)} async-done(((bf16[8,256,512]{2,1,0:T(8,128)(2,1)}), bf16[8,256,512]{2,1,0:T(8,128)(2,1)S(1)}, u32[]{:S(2)}, u32[]{:S(2)}) %all-to-all-start) | async-done | bytes 2097184 | tf_op jit(solution)/shard_map/all_to_all | solution.py:141
  313.2 1.2 copy.19
  314.4 0.8 convolution_convert_fusion
  315.2 2.3 reshape.141
  (25 shorter events, 0.8 us)
Async XLA Ops:
  6.5 170.8 %reduce-scatter.3.cloned.1.call-start = ((), (), s32[]{:S(2)}) async-start(), calls=%async_computation.3 | async-start | bytes 20971520 | tf_op jit(solution)/shard_map/reduce_scatter | solution.py:100
  48.4 199.1 %reduce-scatter.5.cloned.1.call-start = ((), (), s32[]{:S(2)}) async-start(), calls=%async_computation.4 | async-start | bytes 5242880 | tf_op jit(solution)/shard_map/reduce_scatter | solution.py:133
  186.5 4.6 %copy-start.4 = (bf16[2048,2048]{1,0:T(8,128)(2,1)S(1)}, bf16[2048,2048]{1,0:T(8,128)(2,1)}, u32[]{:S(2)}) copy-start(bf16[2048,2048]{1,0:T(8,128)(2,1)} %param.13) | copy-start | bytes 25165828
  201.6 0.7 copy-start.2
  201.7 1.0 copy-start.1
  201.7 1.0 copy-start.3
  253.7 1.6 copy-start
  259.5 53.7 %all-to-all-start = ((bf16[8,256,512]{2,1,0:T(8,128)(2,1)}), bf16[8,256,512]{2,1,0:T(8,128)(2,1)S(1)}, u32[]{:S(2)}, u32[]{:S(2)}) async-start(bf16[8,256,512]{2,1,0:T(8,128)(2,1)} %copy.15), calls=%async_computation.2 | async-start | bytes 4194304 | tf_op jit(solution)/shard_map/all_to_all | solution.py:141
Sparse Core Ops, SparseCore 0:
  48.5 128.8 reduce-scatter.2
  201.8 45.5 reduce-scatter.4
where the time goes:
time: 325 us; the launch traced here: 324 us
  waiting for transfers between devices  215 us (66%)
  matrix products  53.8 us (17%)
  other arithmetic  20.1 us (6%)
  between operations  13.5 us (4%)
  local copies, waits for them, and re-layouts  10.5 us (3%)
  blocking collectives  5.76 us (2%)
  starting transfers between devices  5.55 us (2%)
    reduce_scatter x1, waiting for transfers between devices, body(): lax.psum_scatter(partial_value.astype(jnp.bfloat16), 'tp', scatter_dimens...  128 us
    all_to_all x1, waiting for transfers between devices, body(): lax.all_to_all(outgoing.reshape(group_count, rows_tile, lane_cols), 'dom'...  46.1 us
    dot_general x1, matrix products, body(): jnp.dot(tile_rows, fc2_weight, preferred_element_type=jnp.float32)  41.8 us
    reduce_scatter x1, waiting for transfers between devices, body(): lax.psum_scatter(partial_kv.astype(jnp.bfloat16), 'tp', scatter_dimension...  41.4 us
    dot_general x1, matrix products, body(): jnp.dot(normed.reshape(local_tiles * rows_tile, local_width), kv_weight,...  10.5 us
  transfers between devices with their start and end apart: 3, of which 3 were waited for; matrix products, arithmetic and copies ran while one was open for 2% of the time, Pallas kernels for 0%

commit v1 on v0

--- a/solution.py
+++ b/solution.py
@@ -1,6 +1,10 @@
+import functools
+
 import jax
 import jax.numpy as jnp
 from jax import lax
+from jax.experimental import pallas as pl
+from jax.experimental.pallas import tpu as pltpu
 from jax.sharding import PartitionSpec as P
 
 HEAD = 128
@@ -149,9 +153,492 @@
     return placed.reshape(pre_tiles * rows_tile, lane_cols)
 
 
+ROW_CHUNKS = 4
+COL_CHUNKS = 8
+W_SLOTS = 3
+C_SLOTS = 4
+Y_SLOTS = 8
+LAG = 4
+E_LAG = 1
+F_LAG = 4
+
+
+def fused_kernel(
+    groups,
+    requests,
+    x,
+    w,
+    b2,
+    gain,
+    kvw,
+    kvb,
+    tpr,
+    rg,
+    tl,
+    freq,
+    out,
+    xbuf,
+    wbuf,
+    kvbuf,
+    b2f,
+    gf,
+    kvbf,
+    csend,
+    crecv,
+    own,
+    ysend,
+    yrecv,
+    mine,
+    kvacc,
+    sqacc,
+    kcsend,
+    kcrecv,
+    kysend,
+    kyrecv,
+    kmine,
+    sqsend,
+    sqcrecv,
+    sqysend,
+    sqyrecv,
+    cos_t,
+    sin_t,
+    asend,
+    arecv,
+    xsem,
+    wsem,
+    kvsem,
+    cs_sem,
+    cr_sem,
+    ys_sem,
+    yr_sem,
+    ks_sem,
+    kr_sem,
+    kys_sem,
+    kyr_sem,
+    as_sem,
+    ar_sem,
+):
+    tiles, rows_tile, width = x.shape
+    R, S = ROW_CHUNKS, COL_CHUNKS
+    N = R * S
+    sub = rows_tile // R
+    M = tiles * sub
+    model = w.shape[1]
+    wc = width // S
+    kc = kvw.shape[1] // 4
+    t = lax.axis_index("tp")
+    d = lax.axis_index("dom")
+    c = lax.rem(t, 2)
+    y = t // 2
+    sib = t + 1 - 2 * c
+    opp = t + 2 - 4 * y
+    oy, oc = 1 - y, 1 - c
+    owners = (2 * oy + oc, 2 * y + oc, 2 * oy + c, t)
+    f32, bf16 = jnp.float32, jnp.bfloat16
+
+    def x_copies(r):
+        return [
+            pltpu.make_async_copy(
+                x.at[j, pl.ds(r * sub, sub), :], xbuf.at[r, pl.ds(j * sub, sub), :], xsem.at[r, j]
+            )
+            for j in range(tiles)
+        ]
+
+    def w_copies(n):
+        s = lax.rem(n, S)
+        slot = lax.rem(n, W_SLOTS)
+        return [
+            pltpu.make_async_copy(
+                w.at[:, pl.ds(pl.multiple_of(owners[p] * width + s * wc, wc), wc)],
+                wbuf.at[slot, p],
+                wsem.at[slot, p],
+            )
+            for p in range(4)
+        ]
+
+    def kv_copies():
+        return [
+            pltpu.make_async_copy(
+                kvw.at[:, pl.ds(pl.multiple_of(owners[p] * kc, kc), kc)],
+                kvbuf.at[p],
+                kvsem.at[p],
+            )
+            for p in range(4)
+        ]
+
+    for cp in x_copies(0):
+        cp.start()
+    for n in range(W_SLOTS):
+        for cp in w_copies(jnp.int32(n)):
+            cp.start()
+    for r in range(1, R):
+        for cp in x_copies(r):
+            cp.start()
+    for cp in kv_copies():
+        cp.start()
+
+    barrier = pltpu.get_barrier_semaphore()
+    pl.semaphore_signal(barrier, inc=1, device_id={"tp": sib}, device_id_type=pl.DeviceIdType.MESH)
+    pl.semaphore_signal(barrier, inc=1, device_id={"tp": opp}, device_id_type=pl.DeviceIdType.MESH)
+    for k in range(1, groups):
+        pl.semaphore_signal(
+            barrier,
+            inc=1,
+            device_id={"dom": lax.rem(d + k, groups)},
+            device_id_type=pl.DeviceIdType.MESH,
+        )
+
+    b2f[...] = b2[...].astype(f32)
+    gf[...] = gain[...].astype(f32)
+    kvbf[...] = kvb[...].astype(f32)
+
+    tile_group = []
+    tile_base = []
+    for j in range(tiles):
+        tid = j * groups + d
+        end = jnp.int32(0)
+        grp = jnp.int32(0)
+        base = jnp.int32(0)
+        for q in range(requests):
+            start = end
+            end = end + tpr[q]
+            hit = jnp.logical_and(start <= tid, tid < end)
+            grp = grp + jnp.where(hit, rg[q], 0)
+            base = base + jnp.where(hit, tl[q] + (tid - start) * rows_tile, 0)
+        tile_group.append(grp)
+        tile_base.append(base)
+    first = jnp.int32(0)
+    count = jnp.int32(0)
+    for q in range(requests):
+        first = first + jnp.where(rg[q] < d, tpr[q], 0)
+        count = count + jnp.where(rg[q] == d, tpr[q], 0)
+    is_key = (t * kc < 2 * kc).astype(jnp.int32)
+
+    def remote(src, dst, send, recv, axis, target):
+        return pltpu.make_async_remote_copy(
+            src_ref=src,
+            dst_ref=dst,
+            send_sem=send,
+            recv_sem=recv,
+            device_id={axis: target},
+            device_id_type=pl.DeviceIdType.MESH,
+        )
+
+    def c_copy(n):
+        slot = lax.rem(n, C_SLOTS)
+        return remote(csend.at[slot], crecv.at[n], cs_sem.at[slot], cr_sem.at[n], "tp", sib)
+
+    def y_copy(n):
+        slot = lax.rem(n, Y_SLOTS)
+        return remote(ysend.at[slot], yrecv.at[n], ys_sem.at[slot], yr_sem.at[n], "tp", opp)
+
+    def kc_copy(r):
+        return remote(kcsend.at[r], kcrecv.at[r], ks_sem.at[0, r], kr_sem.at[0, r], "tp", sib)
+
+    def sqc_copy(r):
+        return remote(sqsend.at[r], sqcrecv.at[r], ks_sem.at[1, r], kr_sem.at[1, r], "tp", sib)
+
+    def ky_copy(r):
+        return remote(kysend.at[r], kyrecv.at[r], kys_sem.at[0, r], kyr_sem.at[0, r], "tp", opp)
+
+    def sqy_copy(r):
+        return remote(sqysend.at[r], sqyrecv.at[r], kys_sem.at[1, r], kyr_sem.at[1, r], "tp", opp)
+
+    def a_send(r, k):
+        return remote(
+            asend.at[r, k],
+            arecv.at[d, pl.ds(pl.multiple_of(r * sub, sub), sub), :],
+            as_sem.at[r, k],
+            ar_sem.at[r, k],
+            "dom",
+            lax.rem(d + k, groups),
+        )
+
+    def a_recv(r, k):
+        return remote(
+            asend.at[r, k],
+            arecv.at[lax.rem(d + groups - k, groups), pl.ds(pl.multiple_of(r * sub, sub), sub), :],
+            as_sem.at[r, k],
+            ar_sem.at[r, k],
+            "dom",
+            lax.rem(d + k, groups),
+        )
+
+    def stage_a(n):
+        r, s = n // S, lax.rem(n, S)
+        slot, cslot, oslot = lax.rem(n, W_SLOTS), lax.rem(n, C_SLOTS), lax.rem(n, 2)
+
+        @pl.when(s == 0)
+        def _():
+            for cp in x_copies(r):
+                cp.wait()
+
+        @pl.when(n >= C_SLOTS)
+        def _():
+            c_copy(n - C_SLOTS).wait_send()
+
+        copies = w_copies(n)
+        for p in range(2):
+            copies[p].wait()
+            csend[cslot, p] = jnp.dot(
+                xbuf[r], wbuf[slot, p], preferred_element_type=f32
+            ).astype(bf16)
+        @pl.when(n == 0)
+        def _():
+            pl.semaphore_wait(barrier, groups + 1)
+
+        c_copy(n).start()
+        for p in range(2):
+            copies[2 + p].wait()
+            own[oslot, p] = jnp.dot(xbuf[r], wbuf[slot, 2 + p], preferred_element_type=f32)
+
+        @pl.when(n + W_SLOTS < N)
+        def _():
+            for cp in w_copies(n + W_SLOTS):
+                cp.start()
+
+        @pl.when(s == 1)
+        def _():
+            for j in range(tiles):
+                rows = lax.broadcasted_iota(jnp.int32, (sub, HEAD), 0) + r * sub
+                pos = (rows + tile_base[j]).astype(f32)
+                angle = pos * freq[0:1, :]
+                key = jnp.full((sub, HEAD), is_key, jnp.int32) == 1
+                lane = lax.broadcasted_iota(jnp.int32, (sub, HEAD), 1)
+                sine = jnp.sin(angle)
+                sine = jnp.where(lane < HEAD // 2, -sine, sine)
+                at = pl.ds(j * sub, sub)
+                cos_t[r, at, :] = jnp.where(key, jnp.cos(angle), 1.0)
+                sin_t[r, at, :] = jnp.where(key, sine, 0.0)
+
+    def stage_b(n):
+        yslot, oslot = lax.rem(n, Y_SLOTS), lax.rem(n, 2)
+
+        @pl.when(n >= Y_SLOTS)
+        def _():
+            y_copy(n - Y_SLOTS).wait_send()
+
+        c_copy(n).wait_recv()
+        ysend[yslot] = (own[oslot, 0] + crecv[n, 0].astype(f32)).astype(bf16)
+        y_copy(n).start()
+        mine[yslot] = own[oslot, 1] + crecv[n, 1].astype(f32)
+
+    def stage_c(n):
+        s = lax.rem(n, S)
+        yslot = lax.rem(n, Y_SLOTS)
+
+        @pl.when(n == 0)
+        def _():
+            for cp in kv_copies():
+                cp.wait()
+
+        @pl.when(s == 0)
+        def _():
+            kvacc[...] = jnp.zeros_like(kvacc)
+            sqacc[...] = jnp.zeros_like(sqacc)
+
+        cols = pl.ds(pl.multiple_of(t * width + s * wc, wc), wc)
+        bias = b2f[0:1, cols]
+        scale = gf[0:1, cols]
+        y_copy(n).wait_recv()
+        proj = (mine[yslot] + yrecv[n].astype(f32) + bias).astype(bf16).astype(f32)
+        sq = proj * proj
+        total = sq[:, 0:128]
+        for at in range(128, wc, 128):
+            total = total + sq[:, at : at + 128]
+        sqacc[...] += total
+        u = (proj * scale).astype(bf16)
+        at = pl.ds(pl.multiple_of(s * wc, wc), wc)
+        for p in range(4):
+            kvacc[p] += jnp.dot(u, kvbuf[p, at, :], preferred_element_type=f32)
+
+    def stage_d(r):
+        for p in range(2):
+            kcsend[r, p] = kvacc[p].astype(bf16)
+        kc_copy(r).start()
+        row_sum = jnp.sum(sqacc[...], axis=1, keepdims=True)
+        sqsend[r] = jnp.broadcast_to(row_sum, (M, 128)).T[0:8, :]
+        sqc_copy(r).start()
+        kmine[0] = kvacc[2]
+        kmine[1] = kvacc[3]
+
+    def stage_e(r):
+        kc_copy(r).wait_recv()
+        kysend[r] = (kmine[0] + kcrecv[r, 0].astype(f32)).astype(bf16)
+        ky_copy(r).start()
+        sqc_copy(r).wait_recv()
+        sqysend[r] = sqsend[r] + sqcrecv[r]
+        sqy_copy(r).start()
+        kmine[1] = kmine[1] + kcrecv[r, 1].astype(f32)
+
+    def stage_f(r):
+        sqy_copy(r).wait_recv()
+        total = (sqysend[r] + sqyrecv[r])[0:1, :]
+        norm = lax.rsqrt(jnp.broadcast_to(total, (128, M)).T * (1.0 / model) + EPS)
+        ky_copy(r).wait_recv()
+        cosine, sine = cos_t[r], sin_t[r]
+        heads = []
+        for h in range(kc // HEAD):
+            at = slice(h * HEAD, (h + 1) * HEAD)
+            part = kmine[1, :, at] + kyrecv[r, :, at].astype(f32)
+            kb = kvbf[0:1, pl.ds(pl.multiple_of(t * kc + h * HEAD, HEAD), HEAD)]
+            v = part * norm + kb
+            heads.append(v * cosine + pltpu.roll(v, HEAD // 2, 1) * sine)
+        for k in range(groups):
+            g = lax.rem(d + k, groups)
+            for h in range(kc // HEAD):
+                at = slice(h * HEAD, (h + 1) * HEAD)
+                picked = jnp.zeros((sub, HEAD), f32)
+                for j in range(tiles):
+                    hit = jnp.full((sub, HEAD), tile_group[j], jnp.int32) == g
+                    picked = jnp.where(hit, heads[h][j * sub : (j + 1) * sub, :], picked)
+                asend[r, k, :, at] = picked.astype(bf16)
+            if k > 0:
+                a_send(r, k).start()
+        arecv[d, pl.ds(pl.multiple_of(r * sub, sub), sub), :] = asend[r, 0]
+
+    def step(i, carry):
+        @pl.when(i < N)
+        def _():
+            stage_a(i)
+
+        @pl.when(jnp.logical_and(i >= 1, i <= N))
+        def _():
+            stage_b(i - 1)
+
+        after_d = i - LAG - E_LAG - (S - 1)
+        @pl.when(jnp.logical_and(after_d >= 0, lax.rem(after_d + S * R, S) == 0))
+        def _():
+            stage_e(after_d // S)
+
+        after_e = after_d - F_LAG
+        @pl.when(jnp.logical_and(after_e >= 0, lax.rem(after_e + S * R, S) == 0))
+        def _():
+            stage_f(after_e // S)
+
+        @pl.when(jnp.logical_and(i >= LAG, i < N + LAG))
+        def _():
+            n = i - LAG
+            stage_c(n)
+
+            @pl.when(lax.rem(n, S) == S - 1)
+            def _():
+                stage_d(n // S)
+
+        return carry
+
+    lax.fori_loop(0, N + LAG + E_LAG + F_LAG, step, 0)
+
+    for n in range(N - C_SLOTS, N):
+        c_copy(jnp.int32(n)).wait_send()
+    for n in range(N - Y_SLOTS, N):
+        y_copy(jnp.int32(n)).wait_send()
+    for r in range(R):
+        kc_copy(r).wait_send()
+        sqc_copy(r).wait_send()
+        ky_copy(r).wait_send()
+        sqy_copy(r).wait_send()
+        for k in range(1, groups):
+            a_send(r, k).wait_send()
+    for r in range(R):
+        for k in range(1, groups):
+            a_recv(r, k).wait_recv()
+    for k in range(groups):
+        index = lax.rem(first + k, groups)
+        block = arecv[index].astype(f32)
+        valid = jnp.full(block.shape, count, jnp.int32) > k
+        out[pl.ds(k * rows_tile, rows_tile), :] = jnp.where(valid, block, 0.0).astype(bf16)
+
+
+def fused_body(groups, *args):
+    hidden, w, b2, gain, kvw, kvb, tpr, rg, tl = args
+    tiles, _, rows_tile, width = hidden.shape
+    R, S = ROW_CHUNKS, COL_CHUNKS
+    N = R * S
+    model = w.shape[1]
+    wc = width // S
+    sub = rows_tile // R
+    M = tiles * sub
+    cols = kvw.shape[1]
+    kc = cols // 4
+    half = HEAD // 2
+    freqs = ROPE_BASE ** (-jnp.arange(half, dtype=jnp.float32) * 2.0 / HEAD)
+    freqs = jnp.broadcast_to(jnp.concatenate([freqs, freqs])[None, :], (8, HEAD))
+    f32, bf16 = jnp.float32, jnp.bfloat16
+    any_, vmem, smem = (
+        pl.BlockSpec(memory_space=s) for s in (pl.ANY, pltpu.VMEM, pltpu.SMEM)
+    )
+    V, D = pltpu.VMEM, pltpu.SemaphoreType.DMA
+    rows = 2 * tiles * rows_tile
+    return pl.pallas_call(
+        functools.partial(fused_kernel, groups, tpr.shape[0]),
+        out_shape=jax.ShapeDtypeStruct((rows, kc), bf16),
+        in_specs=[any_, any_, vmem, vmem, any_, vmem, smem, smem, smem, vmem],
+        out_specs=vmem,
+        scratch_shapes=[
+            V((R, M, width), bf16),
+            V((W_SLOTS, 4, width, wc), bf16),
+            V((4, width, kc), bf16),
+            V((1, model), f32),
+            V((1, model), f32),
+            V((1, cols), f32),
+            V((C_SLOTS, 2, M, wc), bf16),
+            V((N, 2, M, wc), bf16),
+            V((2, 2, M, wc), f32),
+            V((Y_SLOTS, M, wc), bf16),
+            V((N, M, wc), bf16),
+            V((Y_SLOTS, M, wc), f32),
+            V((4, M, kc), f32),
+            V((M, 128), f32),
+            V((R, 2, M, kc), bf16),
+            V((R, 2, M, kc), bf16),
+            V((R, M, kc), bf16),
+            V((R, M, kc), bf16),
+            V((2, M, kc), f32),
+            V((R, 8, M), f32),
+            V((R, 8, M), f32),
+            V((R, 8, M), f32),
+            V((R, 8, M), f32),
+            V((R, M, HEAD), f32),
+            V((R, M, HEAD), f32),
+            V((R, groups, sub, kc), bf16),
+            V((groups, rows_tile, kc), bf16),
+            D((R, tiles)),
+            D((W_SLOTS, 4)),
+            D((4,)),
+            D((C_SLOTS,)),
+            D((N,)),
+            D((Y_SLOTS,)),
+            D((N,)),
+            D((2, R)),
+            D((2, R)),
+            D((2, R)),
+            D((2, R)),
+            D((R, groups)),
+            D((R, groups)),
+        ],
+        compiler_params=pltpu.CompilerParams(
+            collective_id=0, has_side_effects=True, vmem_limit_bytes=63 * 1024 * 1024
+        ),
+    )(
+        hidden.reshape(tiles, rows_tile, width),
+        w,
+        b2.reshape(1, model),
+        gain.reshape(1, model),
+        kvw,
+        kvb.reshape(1, cols),
+        tpr,
+        rg,
+        tl,
+        freqs,
+    )
+
+
 def solution(mesh):
+    groups = mesh.shape["dom"]
+    fused = mesh.shape["tp"] == 4
     return jax.shard_map(
-        body,
+        functools.partial(fused_body, groups) if fused else body,
         mesh=mesh,
         in_specs=(
             P(None, "dom", None, "tp"),

time: 325 us -> 158 us (0.49)
  waiting for transfers between devices: 215 us -> 0 us
  Pallas kernels: 0 us -> 149 us
  matrix products: 53.8 us -> 0 us
  other arithmetic: 20.1 us -> 0.09 us
  between operations: 13.5 us -> 0.01 us
  blocking collectives: 5.76 us -> 0 us
  starting transfers between devices: 5.55 us -> 0 us
    reduce_scatter x2 -> x0, waiting for transfers between devices: 169 us -> none  [the longest x1 128 us: body(): lax.psum_scatter(partial_value.astype(jnp.bfloat16), 'tp', scatter_dimens...]
    pallas_call x0 -> x1, Pallas kernels: none -> 149 us  [fused_body(): pl.pallas_call(functools.partial(fused_kernel, groups, tpr.shape[0]), out...]
    dot_general x4 -> x0, matrix products: 53.8 us -> none  [the longest x1 41.8 us: body(): jnp.dot(tile_rows, fc2_weight, preferred_element_type=jnp.float32)]
    all_to_all x1 -> x0, waiting for transfers between devices: 46.1 us -> none  [body(): lax.all_to_all(outgoing.reshape(group_count, rows_tile, lane_cols), 'dom'...]
    convert_element_type x5 -> x0, other arithmetic: 6.44 us -> none  [the longest x1 3.58 us: body(): normed = (widened * scale * gain_part[None, None, :]).astype(jnp.bfloat16)]
    psum x1 -> x0, blocking collectives: 5.76 us -> none  [body(): squares = lax.psum(jnp.sum(widened * widened, axis=2), 'tp')]
    all_to_all x1 -> x0, starting transfers between devices: 5.51 us -> none  [body(): lax.all_to_all(outgoing.reshape(group_count, rows_tile, lane_cols), 'dom'...]
    reduce_sum x6 -> x0, other arithmetic: 4.58 us -> none  [the longest x1 3.35 us: body(): squares = lax.psum(jnp.sum(widened * widened, axis=2), 'tp')]
  transfers between devices with their start and end apart: 3 -> 0, of which waited for: 3 -> 0; matrix products, arithmetic and copies ran while one was open for 2% -> 0% of each run, Pallas kernels for 0% -> 0%
where the time goes in v1:
time: 158 us; the launch traced here: 157 us
  Pallas kernels  149 us (94%)
  local copies, waits for them, and re-layouts  7.61 us (5%)
    pallas_call x1, Pallas kernels, fused_body(): pl.pallas_call(functools.partial(fused_kernel, groups, tpr.shape[0]), out...  149 us

profile of v1, /device:TPU:0, one launch (start us, length us, event | category | flops | bytes accessed | tf_op | source)
XLA Modules:
  0.0 156.8 jit_solution(4629162681738724436)
XLA Ops:
  0.0 0.1 pad_maximum_fusion
  0.1 0.6 broadcast_in_dim.2.freq
  0.7 1.3 reshape.16.kvb
  2.0 1.3 reshape.14.b2
  3.3 1.3 reshape.15.gain
  4.7 149.1 %shard_map.91 = bf16[2048,512]{1,0:T(8,128)(2,1)} custom-call(bf16[4,256,2048]{2,1,0:T(8,128)(2,1)} %bitcast.1, bf16[2048,8192]{1,0:T(8,128)(2,1)} %w.1, bf16[1,8192]{1,0:T(2,128)(2,1)} %reshape.14.b2, bf16[1,8192]{1,0:T(2,128)(2,1)} %reshape.15.gain, bf16[2048,2048]{1,0:T(8,128)(2,1)} %kvw.1, bf16[1,2048]{1,0:T(2,128)(2,1)} %reshape.16.kvb, s32[16]{0:T(128)} %tpr.1, ...), custom_call_target="tpu_custom_call" | custom-call | tf_op jit(solution)/shard_map/pallas_call | solution.py:573
  153.7 3.0 %copy.11 = bf16[2048,512]{1,0:T(8,128)(2,1)} copy(bf16[2048,512]{1,0:T(8,128)(2,1)} %shard_map.91) | data formatting | bytes 4194304
  (1 shorter events, 0.0 us)

commit v2 on v1

--- a/solution.py
+++ b/solution.py
@@ -158,8 +158,9 @@
 W_SLOTS = 3
 C_SLOTS = 4
 Y_SLOTS = 8
-LAG = 4
+LAG = 5
 E_LAG = 1
+KV_STEPS = (4, 6, 8)
 F_LAG = 4
 
 
@@ -168,10 +169,8 @@
     requests,
     x,
     w,
-    b2,
-    gain,
     kvw,
-    kvb,
+    vecs,
     tpr,
     rg,
     tl,
@@ -180,9 +179,6 @@
     xbuf,
     wbuf,
     kvbuf,
-    b2f,
-    gf,
-    kvbf,
     csend,
     crecv,
     own,
@@ -196,6 +192,7 @@
     kysend,
     kyrecv,
     kmine,
+    ubuf,
     sqsend,
     sqcrecv,
     sqysend,
@@ -226,6 +223,7 @@
     model = w.shape[1]
     wc = width // S
     kc = kvw.shape[1] // 4
+    kh = kc // 2
     t = lax.axis_index("tp")
     d = lax.axis_index("dom")
     c = lax.rem(t, 2)
@@ -250,7 +248,7 @@
         return [
             pltpu.make_async_copy(
                 w.at[:, pl.ds(pl.multiple_of(owners[p] * width + s * wc, wc), wc)],
-                wbuf.at[slot, p],
+                wbuf.at[slot, p // 2, :, pl.ds(p % 2 * wc, wc)],
                 wsem.at[slot, p],
             )
             for p in range(4)
@@ -268,13 +266,7 @@
 
     for cp in x_copies(0):
         cp.start()
-    for n in range(W_SLOTS):
-        for cp in w_copies(jnp.int32(n)):
-            cp.start()
-    for r in range(1, R):
-        for cp in x_copies(r):
-            cp.start()
-    for cp in kv_copies():
+    for cp in w_copies(jnp.int32(0)):
         cp.start()
 
     barrier = pltpu.get_barrier_semaphore()
@@ -287,10 +279,6 @@
             device_id={"dom": lax.rem(d + k, groups)},
             device_id_type=pl.DeviceIdType.MESH,
         )
-
-    b2f[...] = b2[...].astype(f32)
-    gf[...] = gain[...].astype(f32)
-    kvbf[...] = kvb[...].astype(f32)
 
     tile_group = []
     tile_base = []
@@ -338,31 +326,34 @@
     def sqc_copy(r):
         return remote(sqsend.at[r], sqcrecv.at[r], ks_sem.at[1, r], kr_sem.at[1, r], "tp", sib)
 
-    def ky_copy(r):
-        return remote(kysend.at[r], kyrecv.at[r], kys_sem.at[0, r], kyr_sem.at[0, r], "tp", opp)
+    def ky_copy(r, part):
+        return remote(
+            kysend.at[r, part],
+            kyrecv.at[r, part],
+            kys_sem.at[part, r],
+            kyr_sem.at[part, r],
+            "tp",
+            opp,
+        )
 
     def sqy_copy(r):
-        return remote(sqysend.at[r], sqyrecv.at[r], kys_sem.at[1, r], kyr_sem.at[1, r], "tp", opp)
-
-    def a_send(r, k):
+        return remote(sqysend.at[r], sqyrecv.at[r], kys_sem.at[2, r], kyr_sem.at[2, r], "tp", opp)
+
+    def a_copy(r, k, part, origin):
         return remote(
-            asend.at[r, k],
-            arecv.at[d, pl.ds(pl.multiple_of(r * sub, sub), sub), :],
-            as_sem.at[r, k],
-            ar_sem.at[r, k],
+            asend.at[r, part, k],
+            arecv.at[part, origin, pl.ds(pl.multiple_of(r * sub, sub), sub), :],
+            as_sem.at[r, part, k],
+            ar_sem.at[r, part, k],
             "dom",
             lax.rem(d + k, groups),
         )
 
-    def a_recv(r, k):
-        return remote(
-            asend.at[r, k],
-            arecv.at[lax.rem(d + groups - k, groups), pl.ds(pl.multiple_of(r * sub, sub), sub), :],
-            as_sem.at[r, k],
-            ar_sem.at[r, k],
-            "dom",
-            lax.rem(d + k, groups),
-        )
+    def a_send(r, k, part):
+        return a_copy(r, k, part, d)
+
+    def a_recv(r, k, part):
+        return a_copy(r, k, part, lax.rem(d + groups - k, groups))
 
     def stage_a(n):
         r, s = n // S, lax.rem(n, S)
@@ -380,22 +371,44 @@
         copies = w_copies(n)
         for p in range(2):
             copies[p].wait()
-            csend[cslot, p] = jnp.dot(
-                xbuf[r], wbuf[slot, p], preferred_element_type=f32
-            ).astype(bf16)
+        away = jnp.dot(xbuf[r], wbuf[slot, 0], preferred_element_type=f32).astype(bf16)
+        for p in range(2):
+            csend[cslot, p] = away[:, p * wc : (p + 1) * wc]
         @pl.when(n == 0)
         def _():
             pl.semaphore_wait(barrier, groups + 1)
 
         c_copy(n).start()
+
+        @pl.when(n == 0)
+        def _():
+            for cp in w_copies(jnp.int32(1)):
+                cp.start()
+
         for p in range(2):
             copies[2 + p].wait()
-            own[oslot, p] = jnp.dot(xbuf[r], wbuf[slot, 2 + p], preferred_element_type=f32)
+        home = jnp.dot(xbuf[r], wbuf[slot, 1], preferred_element_type=f32)
+        for p in range(2):
+            own[oslot, p] = home[:, p * wc : (p + 1) * wc]
+
+        @pl.when(n == 0)
+        def _():
+            for k in range(2, W_SLOTS):
+                for cp in w_copies(jnp.int32(k)):
+                    cp.start()
 
         @pl.when(n + W_SLOTS < N)
         def _():
             for cp in w_copies(n + W_SLOTS):
                 cp.start()
+
+        @pl.when(n == 1)
+        def _():
+            for cp in kv_copies():
+                cp.start()
+            for k in range(1, R):
+                for cp in x_copies(k):
+                    cp.start()
 
         @pl.when(s == 1)
         def _():
@@ -432,25 +445,37 @@
             for cp in kv_copies():
                 cp.wait()
 
-        @pl.when(s == 0)
-        def _():
-            kvacc[...] = jnp.zeros_like(kvacc)
-            sqacc[...] = jnp.zeros_like(sqacc)
-
         cols = pl.ds(pl.multiple_of(t * width + s * wc, wc), wc)
-        bias = b2f[0:1, cols]
-        scale = gf[0:1, cols]
+        gcols = pl.ds(pl.multiple_of(model + t * width + s * wc, wc), wc)
+        bias = vecs[0:1, cols]
+        scale = vecs[0:1, gcols]
         y_copy(n).wait_recv()
         proj = (mine[yslot] + yrecv[n].astype(f32) + bias).astype(bf16).astype(f32)
         sq = proj * proj
         total = sq[:, 0:128]
         for at in range(128, wc, 128):
             total = total + sq[:, at : at + 128]
+
+        @pl.when(s == 0)
+        def _():
+            sqacc[...] = jnp.zeros_like(sqacc)
+
         sqacc[...] += total
-        u = (proj * scale).astype(bf16)
-        at = pl.ds(pl.multiple_of(s * wc, wc), wc)
-        for p in range(4):
-            kvacc[p] += jnp.dot(u, kvbuf[p, at, :], preferred_element_type=f32)
+        ubuf[s] = (proj * scale).astype(bf16)
+
+        low = 0
+        for high in KV_STEPS:
+
+            @pl.when(s == high - 1)
+            def _(low=low, high=high):
+                u = jnp.concatenate([ubuf[q] for q in range(low, high)], axis=1)
+                for p in range(4):
+                    more = jnp.dot(
+                        u, kvbuf[p, low * wc : high * wc, :], preferred_element_type=f32
+                    )
+                    kvacc[p] = more if low == 0 else kvacc[p] + more
+
+            low = high
 
     def stage_d(r):
         for p in range(2):
@@ -459,43 +484,49 @@
         row_sum = jnp.sum(sqacc[...], axis=1, keepdims=True)
         sqsend[r] = jnp.broadcast_to(row_sum, (M, 128)).T[0:8, :]
         sqc_copy(r).start()
-        kmine[0] = kvacc[2]
-        kmine[1] = kvacc[3]
 
     def stage_e(r):
         kc_copy(r).wait_recv()
-        kysend[r] = (kmine[0] + kcrecv[r, 0].astype(f32)).astype(bf16)
-        ky_copy(r).start()
-        sqc_copy(r).wait_recv()
-        sqysend[r] = sqsend[r] + sqcrecv[r]
-        sqy_copy(r).start()
-        kmine[1] = kmine[1] + kcrecv[r, 1].astype(f32)
+        for part in range(2):
+            at = slice(part * kh, (part + 1) * kh)
+            kysend[r, part] = (kvacc[2, :, at] + kcrecv[r, 0, :, at].astype(f32)).astype(bf16)
+            ky_copy(r, part).start()
+            if part == 0:
+                sqc_copy(r).wait_recv()
+                sqysend[r] = sqsend[r] + sqcrecv[r]
+                sqy_copy(r).start()
+        kmine[...] = kvacc[3] + kcrecv[r, 1].astype(f32)
 
     def stage_f(r):
-        sqy_copy(r).wait_recv()
-        total = (sqysend[r] + sqyrecv[r])[0:1, :]
-        norm = lax.rsqrt(jnp.broadcast_to(total, (128, M)).T * (1.0 / model) + EPS)
-        ky_copy(r).wait_recv()
         cosine, sine = cos_t[r], sin_t[r]
-        heads = []
-        for h in range(kc // HEAD):
-            at = slice(h * HEAD, (h + 1) * HEAD)
-            part = kmine[1, :, at] + kyrecv[r, :, at].astype(f32)
-            kb = kvbf[0:1, pl.ds(pl.multiple_of(t * kc + h * HEAD, HEAD), HEAD)]
-            v = part * norm + kb
-            heads.append(v * cosine + pltpu.roll(v, HEAD // 2, 1) * sine)
-        for k in range(groups):
-            g = lax.rem(d + k, groups)
-            for h in range(kc // HEAD):
-                at = slice(h * HEAD, (h + 1) * HEAD)
-                picked = jnp.zeros((sub, HEAD), f32)
-                for j in range(tiles):
-                    hit = jnp.full((sub, HEAD), tile_group[j], jnp.int32) == g
-                    picked = jnp.where(hit, heads[h][j * sub : (j + 1) * sub, :], picked)
-                asend[r, k, :, at] = picked.astype(bf16)
-            if k > 0:
-                a_send(r, k).start()
-        arecv[d, pl.ds(pl.multiple_of(r * sub, sub), sub), :] = asend[r, 0]
+        rows = pl.ds(pl.multiple_of(r * sub, sub), sub)
+        norm = None
+        for part in range(2):
+            ky_copy(r, part).wait_recv()
+            if part == 0:
+                sqy_copy(r).wait_recv()
+                total = (sqysend[r] + sqyrecv[r])[0:1, :]
+                norm = lax.rsqrt(jnp.broadcast_to(total, (128, M)).T * (1.0 / model) + EPS)
+            heads = []
+            for h in range(kh // HEAD):
+                here = slice(h * HEAD, (h + 1) * HEAD)
+                at = slice(part * kh + h * HEAD, part * kh + (h + 1) * HEAD)
+                sums = kmine[:, at] + kyrecv[r, part, :, here].astype(f32)
+                start = pl.multiple_of(2 * model + t * kc + part * kh + h * HEAD, HEAD)
+                v = sums * norm + vecs[0:1, pl.ds(start, HEAD)]
+                heads.append(v * cosine + pltpu.roll(v, HEAD // 2, 1) * sine)
+            for k in list(range(1, groups)) + [0]:
+                g = lax.rem(d + k, groups)
+                for h in range(kh // HEAD):
+                    here = slice(h * HEAD, (h + 1) * HEAD)
+                    picked = jnp.zeros((sub, HEAD), f32)
+                    for j in range(tiles):
+                        hit = jnp.full((sub, HEAD), tile_group[j], jnp.int32) == g
+                        picked = jnp.where(hit, heads[h][j * sub : (j + 1) * sub, :], picked)
+                    asend[r, part, k, :, here] = picked.astype(bf16)
+                if k > 0:
+                    a_send(r, k, part).start()
+            arecv[part, d, rows, :] = asend[r, part, 0]
 
     def step(i, carry):
         @pl.when(i < N)
@@ -536,18 +567,22 @@
     for r in range(R):
         kc_copy(r).wait_send()
         sqc_copy(r).wait_send()
-        ky_copy(r).wait_send()
         sqy_copy(r).wait_send()
-        for k in range(1, groups):
-            a_send(r, k).wait_send()
+        for part in range(2):
+            ky_copy(r, part).wait_send()
+            for k in range(1, groups):
+                a_send(r, k, part).wait_send()
     for r in range(R):
-        for k in range(1, groups):
-            a_recv(r, k).wait_recv()
+        for part in range(2):
+            for k in range(1, groups):
+                a_recv(r, k, part).wait_recv()
     for k in range(groups):
         index = lax.rem(first + k, groups)
-        block = arecv[index].astype(f32)
-        valid = jnp.full(block.shape, count, jnp.int32) > k
-        out[pl.ds(k * rows_tile, rows_tile), :] = jnp.where(valid, block, 0.0).astype(bf16)
+        for part in range(2):
+            block = arecv[part, index].astype(f32)
+            valid = jnp.full(block.shape, count, jnp.int32) > k
+            at = slice(part * kh, (part + 1) * kh)
+            out[pl.ds(k * rows_tile, rows_tile), at] = jnp.where(valid, block, 0.0).astype(bf16)
 
 
 def fused_body(groups, *args):
@@ -561,6 +596,7 @@
     M = tiles * sub
     cols = kvw.shape[1]
     kc = cols // 4
+    kh = kc // 2
     half = HEAD // 2
     freqs = ROPE_BASE ** (-jnp.arange(half, dtype=jnp.float32) * 2.0 / HEAD)
     freqs = jnp.broadcast_to(jnp.concatenate([freqs, freqs])[None, :], (8, HEAD))
@@ -573,15 +609,12 @@
     return pl.pallas_call(
         functools.partial(fused_kernel, groups, tpr.shape[0]),
         out_shape=jax.ShapeDtypeStruct((rows, kc), bf16),
-        in_specs=[any_, any_, vmem, vmem, any_, vmem, smem, smem, smem, vmem],
+        in_specs=[any_, any_, any_, vmem, smem, smem, smem, vmem],
         out_specs=vmem,
         scratch_shapes=[
             V((R, M, width), bf16),
-            V((W_SLOTS, 4, width, wc), bf16),
+            V((W_SLOTS, 2, width, 2 * wc), bf16),
             V((4, width, kc), bf16),
-            V((1, model), f32),
-            V((1, model), f32),
-            V((1, cols), f32),
             V((C_SLOTS, 2, M, wc), bf16),
             V((N, 2, M, wc), bf16),
             V((2, 2, M, wc), f32),
@@ -592,17 +625,18 @@
             V((M, 128), f32),
             V((R, 2, M, kc), bf16),
             V((R, 2, M, kc), bf16),
-            V((R, M, kc), bf16),
-            V((R, M, kc), bf16),
-            V((2, M, kc), f32),
+            V((R, 2, M, kh), bf16),
+            V((R, 2, M, kh), bf16),
+            V((M, kc), f32),
+            V((S, M, wc), bf16),
             V((R, 8, M), f32),
             V((R, 8, M), f32),
             V((R, 8, M), f32),
             V((R, 8, M), f32),
             V((R, M, HEAD), f32),
             V((R, M, HEAD), f32),
-            V((R, groups, sub, kc), bf16),
-            V((groups, rows_tile, kc), bf16),
+            V((R, 2, groups, sub, kh), bf16),
+            V((2, groups, rows_tile, kh), bf16),
             D((R, tiles)),
             D((W_SLOTS, 4)),
             D((4,)),
@@ -612,10 +646,10 @@
             D((N,)),
             D((2, R)),
             D((2, R)),
-            D((2, R)),
-            D((2, R)),
-            D((R, groups)),
-            D((R, groups)),
+            D((3, R)),
+            D((3, R)),
+            D((R, 2, groups)),
+            D((R, 2, groups)),
         ],
         compiler_params=pltpu.CompilerParams(
             collective_id=0, has_side_effects=True, vmem_limit_bytes=63 * 1024 * 1024
@@ -623,10 +657,8 @@
     )(
         hidden.reshape(tiles, rows_tile, width),
         w,
-        b2.reshape(1, model),
-        gain.reshape(1, model),
         kvw,
-        kvb.reshape(1, cols),
+        jnp.concatenate([b2, gain, kvb]).astype(f32).reshape(1, 2 * model + cols),
         tpr,
         rg,
         tl,

time: 158 us -> 150 us (0.949)
  Pallas kernels: 149 us -> 143 us
  local copies, waits for them, and re-layouts: 7.61 us -> 5.82 us
    pallas_call x1, Pallas kernels: 149 us -> 143 us  [fused_body(): pl.pallas_call(functools.partial(fused_kernel, groups, tpr.shape[0]), out...]
    reshape x3 -> x0, local copies, waits for them, and re-layouts: 3.97 us -> none  [the longest x1 1.35 us: fused_body(): b2.reshape(1, model)]
    concatenate x0 -> x3, local copies, waits for them, and re-layouts: none -> 2.17 us  [fused_body(): jnp.concatenate([b2, gain, kvb]).astype(f32).reshape(1, 2 * model + cols)]
where the time goes in v2:
time: 150 us; the launch traced here: 149 us
  Pallas kernels  143 us (95%)
  local copies, waits for them, and re-layouts  5.82 us (4%)
    pallas_call x1, Pallas kernels, fused_body(): pl.pallas_call(functools.partial(fused_kernel, groups, tpr.shape[0]), out...  143 us
    unnamed x1, local copies, waits for them, and re-layouts  3.05 us

profile of v2, /device:TPU:0, one launch (start us, length us, event | category | flops | bytes accessed | tf_op | source)
XLA Modules:
  0.0 149.3 jit_solution(16218868033324275161)
XLA Ops:
  0.0 0.1 pad_maximum_fusion
  0.1 0.6 broadcast_in_dim.2.freq
  0.7 0.7 concatenate.21
  1.4 0.7 concatenate.19
  2.1 0.7 concatenate.20
  2.9 0.7 maximum_convert_fusion.vecs
  3.6 142.7 %shard_map.91 = bf16[2048,512]{1,0:T(8,128)(2,1)} custom-call(bf16[4,256,2048]{2,1,0:T(8,128)(2,1)} %bitcast.1, bf16[2048,8192]{1,0:T(8,128)(2,1)} %w.1, bf16[2048,2048]{1,0:T(8,128)(2,1)} %kvw.1, f32[1,18432]{1,0:T(1,128)} %maximum_convert_fusion.vecs, s32[16]{0:T(128)} %tpr.1, s32[16]{0:T(128)} %rg.1, s32[16]{0:T(128)} %tl.1, f32[8,128]{1,0:T(8,128)} %broadcast_in_dim.2.freq), custom_call_target="tpu_custom_call" | custom-call | tf_op jit(solution)/shard_map/pallas_call | solution.py:609
  146.3 3.0 %copy.11 = bf16[2048,512]{1,0:T(8,128)(2,1)} copy(bf16[2048,512]{1,0:T(8,128)(2,1)} %shard_map.91) | data formatting | bytes 4194304
  (1 shorter events, 0.0 us)
